TPU v7x, 32 devices: a whole 2x2x4 slice. The times are simulated.
32 devices in a mesh: vis: 16 (over z, y, x), chan: 2 (over core).
Axes of the slice: x: 2, y: 2, z: 4, core: 2. Of those that a mesh axis runs over, the one named last changes fastest.
Arguments:
- model: float32 [2, 64, 1024], P(None, 'vis', 'chan'), may hold values from -6 to 6
- kernels: float32 [2, 32, 8], replicated, may hold values from -1.5 to 1.5
- vis_data: float32 [2, 2, 131072], P(None, 'chan', 'vis'), may hold values from -6 to 6
- vis_weight: float32 [2, 131072], P('chan', 'vis'), may hold values from 0.2 to 2
- tile_list: int32 [2, 16, 16], P('chan', 'vis'), may hold values from 0 to 63, as said below
- vis_slot: int32 [2, 131072], P('chan', 'vis'), may hold values from 0 to 15
- vis_wplane: int32 [2, 131072], P('chan', 'vis'), may hold values from 0 to 31
- vis_offset: int32 [2, 2, 131072], P(None, 'chan', 'vis'), may hold values from 0 to 24
Outputs:
- model_step: float32 [2, 64, 1024], P(None, 'vis', 'chan')
- residual: float32 [2, 2, 131072], P(None, 'chan', 'vis')
Inputs may be any that keep to these rules, and one draw needn't show every extreme that they name: `tile_list`: the 16 tiles of one block's list are different and have different owners t // 4.
All inputs are finite; a program needn't handle non-finite values.
Results may differ from a plain program's by a relative error of at most 0.0003.
Values sent between devices are 32-bit elements; how exact they have to be, the bound alone decides.
A program may use at most 64 MiB of HBM per device.

v0:
```python
import math

import jax
import jax.numpy as jnp
from jax import lax
from jax.sharding import PartitionSpec as P

TILE_SIDE = 32


HIGH = lax.Precision.HIGHEST


def dft_tables(side):
    index = jnp.arange(side, dtype=jnp.int32)
    angle = 2.0 * math.pi / side * (index[:, None] * index[None, :] % side).astype(jnp.float32)
    scale = 1.0 / math.sqrt(side)
    return (jnp.cos(angle) * scale, -jnp.sin(angle) * scale)


def forward(images, cosine, sine):

    def triple(left, right):
        return jnp.einsum("pa,tab,bq->tqp", left, images, right, precision=HIGH)

    return (
        triple(cosine, cosine) - triple(sine, sine),
        triple(cosine, sine) + triple(sine, cosine),
    )


def adjoint(part_re, part_im, cosine, sine):

    def triple(left, middle, right):
        return jnp.einsum("ap,tqp,qb->tab", left, middle, right, precision=HIGH)

    return (
        triple(cosine, part_re, cosine)
        - triple(sine, part_re, sine)
        + triple(sine, part_im, cosine)
        + triple(cosine, part_im, sine)
    )


def place(offset, taps, side):
    rows = jnp.arange(side, dtype=jnp.int32)[:, None]
    shift = rows - offset[None, :]
    total = jnp.zeros((side, offset.shape[0]), jnp.float32)
    for tap in range(taps.shape[0]):
        total = total + jnp.where(shift == tap, taps[tap][None, :], jnp.float32(0.0))
    return total


def crossed(left, right):
    return lax.dot_general(left, right, (((1,), (1,)), ((), ())), precision=HIGH)


def visibility_pass(
    grid_re, grid_im, slot, wplane, off_u, off_v, data_re, data_im, weight, kernels
):
    slots, side = (grid_re.shape[0], grid_re.shape[1])
    planes = kernels.shape[1]
    picker = (jnp.arange(planes, dtype=jnp.int32)[:, None] == wplane[None, :]).astype(jnp.float32)
    taps_re = jnp.dot(kernels[0].T, picker, precision=HIGH)
    taps_im = jnp.dot(kernels[1].T, picker, precision=HIGH)
    a_re = place(off_u, taps_re, side)
    a_im = place(off_u, taps_im, side)
    b_re = place(off_v, taps_re, side)
    b_im = place(off_v, taps_im, side)
    flat_re = grid_re.reshape(slots * side, side)
    flat_im = grid_im.reshape(slots * side, side)
    y_re = jnp.dot(flat_re, a_re, precision=HIGH) - jnp.dot(flat_im, a_im, precision=HIGH)
    y_im = jnp.dot(flat_re, a_im, precision=HIGH) + jnp.dot(flat_im, a_re, precision=HIGH)
    y_re = y_re.reshape(slots, side, -1)
    y_im = y_im.reshape(slots, side, -1)
    owner = (jnp.arange(slots, dtype=jnp.int32)[:, None] == slot[None, :]).astype(jnp.float32)
    pred_re = jnp.sum(owner * jnp.sum(y_re * b_re[None] - y_im * b_im[None], axis=1), axis=0)
    pred_im = jnp.sum(owner * jnp.sum(y_re * b_im[None] + y_im * b_re[None], axis=1), axis=0)
    res_re = weight * (data_re - pred_re)
    res_im = weight * (data_im - pred_im)
    z_re = (owner[:, None, :] * (res_re * b_re + res_im * b_im)[None]).reshape(slots * side, -1)
    z_im = (owner[:, None, :] * (res_im * b_re - res_re * b_im)[None]).reshape(slots * side, -1)
    part_re = crossed(z_re, a_re) + crossed(z_im, a_im)
    part_im = crossed(z_im, a_re) - crossed(z_re, a_im)
    return (res_re, res_im, part_re.reshape(slots, side, side), part_im.reshape(slots, side, side))


def shards(model, kernels, vis_data, vis_weight, tile_list, vis_slot, vis_wplane, vis_offset):
    side = TILE_SIDE
    cells = side * side
    channels = lax.axis_size("chan")
    chan_here = lax.axis_index("chan")
    offsets_all = (jnp.arange(channels, dtype=jnp.float32) - 0.5 * (channels - 1)) / channels
    frequency = jnp.sum(
        jnp.where(jnp.arange(channels, dtype=jnp.int32) == chan_here, offsets_all, jnp.float32(0.0))
    )
    cosine, sine = dft_tables(side)
    listed = tile_list[0, 0]
    slots = listed.shape[0]
    tile_dev = model.shape[1]
    piece_cells = model.shape[2]
    whole = lax.all_gather(model, "chan", axis=2, tiled=True)

    def matches(length):
        return (listed[:, None] == jnp.arange(length, dtype=jnp.int32)[None, :]).astype(jnp.float32)

    image = (whole[0] + frequency * whole[1]).reshape(tile_dev, side, side)
    own_re, own_im = forward(image, cosine, sine)
    packed = jnp.concatenate(
        [own_re.reshape(tile_dev, cells), own_im.reshape(tile_dev, cells)], axis=1
    )
    piece = lax.all_gather(packed, "vis", axis=0, tiled=True)
    chosen = jnp.dot(matches(piece.shape[0]), piece, precision=HIGH)
    grid_re = chosen[:, :cells].reshape(slots, side, side)
    grid_im = chosen[:, cells:].reshape(slots, side, side)
    count = vis_data.shape[2]
    block = min(512, count)
    blocks = count // block

    def rows_of(values):
        return values.reshape(blocks, block)

    sequence = (
        rows_of(vis_slot[0]),
        rows_of(vis_wplane[0]),
        rows_of(vis_offset[0, 0]),
        rows_of(vis_offset[1, 0]),
        rows_of(vis_data[0, 0]),
        rows_of(vis_data[1, 0]),
        rows_of(vis_weight[0]),
    )

    def one_block(carry, inputs):
        slot, wplane, off_u, off_v, data_re, data_im, weight = inputs
        res_re, res_im, part_re, part_im = visibility_pass(
            grid_re, grid_im, slot, wplane, off_u, off_v, data_re, data_im, weight, kernels
        )
        return ((carry[0] + part_re, carry[1] + part_im), (res_re, res_im))

    empty = jnp.zeros((slots, side, side), jnp.float32)
    (acc_re, acc_im), (out_re, out_im) = lax.scan(one_block, (empty, empty), sequence)
    residual = jnp.stack([out_re.reshape(count), out_im.reshape(count)])[:, None, :]
    partial_tiles = jnp.concatenate(
        [acc_re.reshape(slots, cells), acc_im.reshape(slots, cells)], axis=1
    )
    owned = lax.psum_scatter(
        jnp.dot(matches(lax.axis_size("vis") * tile_dev).T, partial_tiles, precision=HIGH),
        "vis",
        scatter_dimension=0,
        tiled=True,
    )
    dirty = adjoint(
        owned[:, :cells].reshape(tile_dev, side, side),
        owned[:, cells:].reshape(tile_dev, side, side),
        cosine,
        sine,
    ).reshape(tile_dev, cells)
    every = lax.all_gather(dirty[None], "chan", axis=0, tiled=True)
    mine = lax.dynamic_slice_in_dim(every, chan_here * piece_cells, piece_cells, 2)
    gradient = jnp.stack(
        [jnp.sum(mine, axis=0), jnp.sum(offsets_all[:, None, None] * mine, axis=0)]
    )
    curvature = jnp.stack([jnp.float32(channels), jnp.sum(offsets_all * offsets_all)])
    model_step = gradient / curvature[:, None, None]
    return (model_step, residual)


def solution(mesh):
    placed = (
        P(None, "vis", "chan"),
        P(),
        P(None, "chan", "vis"),
        P("chan", "vis"),
        P("chan", "vis", None),
        P("chan", "vis"),
        P("chan", "vis"),
        P(None, "chan", "vis"),
    )
    return jax.shard_map(
        shards,
        mesh=mesh,
        in_specs=placed,
        out_specs=(P(None, "vis", "chan"), P(None, "chan", "vis")),
        check_vma=False,
    )
```

profile of v0, /device:TPU:0, one launch (start us, length us, event | category | flops | bytes accessed | tf_op | source)
XLA Modules:
  0.0 358.7 jit_solution(10396690389444094372)
XLA Ops:
  7.8 2.3 all_gather.9
  13.0 45.4 %all-gather = f32[16,4,2048]{2,1,0:T(4,128)S(1)} all-gather(f32[1,4,2048]{2,1,0:T(4,128)S(1)} %maximum_bitcast_fusion), channel_id=1, replica_groups=mesh['vis'=16,'chan'=2] {'vis'}, dimensions={0}, use_global_device_ids=true | all-gather | bytes 557056 | tf_op jit(solution)/shard_map/all_gather | solution.py:112
  66.8 172.2 %while.17 = (s32[]{:T(128)}, f32[16,32,32]{1,0,2:T(8,128)S(1)}, f32[16,32,32]{1,0,2:T(8,128)S(1)}, f32[16,512]{1,0:T(8,128)S(1)}, f32[16,512]{1,0:T(8,128)S(1)},...) while((s32[]{:T(128)}, f32[16,32,32]{1,0,2:T(8,128)S(1)}, ...), condition=%wide.region_6.7_spmd.clone, body=%wide.region_1.6_spmd.clone.sunk | while | flops 816292864 | bytes 15255747 | solution.py:141
  70.6 1.5 subtract_reduce_fusion.2
  73.7 1.1 convolution_add_fusion.6
  76.0 1.1 convolution_subtract_fusion.7
  81.4 1.5 subtract_reduce_fusion.2
  83.3 1.1 fusion.270
  84.4 1.1 convolution_add_fusion.6
  86.7 1.1 convolution_subtract_fusion.7
  92.1 1.5 subtract_reduce_fusion.2
  94.1 1.1 fusion.270
  95.2 1.1 convolution_add_fusion.6
  97.5 1.1 convolution_subtract_fusion.7
  102.9 1.5 subtract_reduce_fusion.2
  104.8 1.1 fusion.270
  105.9 1.1 convolution_add_fusion.6
  108.3 1.1 convolution_subtract_fusion.7
  113.6 1.5 subtract_reduce_fusion.2
  115.6 1.1 fusion.270
  116.7 1.1 convolution_add_fusion.6
  119.0 1.1 convolution_subtract_fusion.7
  124.4 1.5 subtract_reduce_fusion.2
  126.4 1.1 fusion.270
  127.5 1.1 convolution_add_fusion.6
  129.8 1.1 convolution_subtract_fusion.7
  135.2 1.5 subtract_reduce_fusion.2
  137.1 1.1 fusion.270
  138.2 1.1 convolution_add_fusion.6
  140.6 1.1 convolution_subtract_fusion.7
  145.9 1.5 subtract_reduce_fusion.2
  147.9 1.1 fusion.270
  149.0 1.1 convolution_add_fusion.6
  151.3 1.1 convolution_subtract_fusion.7
  156.7 1.5 subtract_reduce_fusion.2
  158.7 1.1 fusion.270
  159.7 1.1 convolution_add_fusion.6
  162.1 1.1 convolution_subtract_fusion.7
  167.5 1.5 subtract_reduce_fusion.2
  169.4 1.1 fusion.270
  170.5 1.1 convolution_add_fusion.6
  172.8 1.1 convolution_subtract_fusion.7
  178.2 1.5 subtract_reduce_fusion.2
  181.3 1.1 convolution_add_fusion.6
  183.6 1.1 convolution_subtract_fusion.7
  189.0 1.5 subtract_reduce_fusion.2
  192.0 1.1 convolution_add_fusion.6
  194.4 1.1 convolution_subtract_fusion.7
  199.7 1.5 subtract_reduce_fusion.2
  202.8 1.1 convolution_add_fusion.6
  205.1 1.1 convolution_subtract_fusion.7
  210.5 1.5 subtract_reduce_fusion.2
  212.5 1.1 fusion.270
  213.6 1.1 convolution_add_fusion.6
  215.9 1.1 convolution_subtract_fusion.7
  221.3 1.5 subtract_reduce_fusion.2
  224.3 1.1 convolution_add_fusion.6
  226.7 1.1 convolution_subtract_fusion.7
  232.0 1.5 subtract_reduce_fusion.2
  235.1 1.1 convolution_add_fusion.6
  237.4 1.1 convolution_subtract_fusion.7
  239.6 1.3 fusion.101
  245.0 100.3 %all-reduce.3.cloned.1.call-done = f32[64,2048]{1,0:T(8,128)} async-done(((f32[64,2048]{1,0:T(8,128)}), f32[64,2048]{1,0:T(8,128)}) %all-reduce.3.cloned.1.call-update) | async-done | bytes 524304
  349.2 1.8 all_gather.11
  (485 shorter events, 118.9 us)
Async XLA Ops:
  7.2 338.1 %all-reduce.3.cloned.1.call-start = ((), (), s32[]{:S(2)}) async-start(), calls=%async_computation | async-start | bytes 1048576
  58.6 0.7 copy-start.6
  59.6 0.8 copy-start.1
  60.6 0.8 copy-start.2
  61.6 0.8 copy-start.3
  63.1 0.8 copy-start.4
  64.6 0.8 copy-start.5
  66.1 0.7 copy-start
  241.7 0.7 copy-start.7
Sparse Core Ops, SparseCore 0:
  241.0 104.1 all-reduce.2
where the time goes:
time: 359 us
  matrix products  154 us (43%)
  waiting for transfers between devices  100 us (28%)
  blocking collectives  49.6 us (14%)
  local copies, waits for them, and re-layouts  20.4 us (6%)
  other arithmetic  16.2 us (5%)
  between operations  15 us (4%)
    unnamed x2, waiting for transfers between devices  100 us
    dot_general x64, matrix products, crossed(): lax.dot_general(left, right, (((1,), (1,)), ((), ())), precision=HIGH)  70.7 us
    all_gather x1, blocking collectives, shards(): piece = lax.all_gather(packed, 'vis', axis=0, tiled=True)  45.4 us
    dot_general x16, matrix products, visibility_pass(): jnp.dot(flat_im, a_re, precision=HIGH)  23.7 us
    dot_general x16, matrix products, visibility_pass(): jnp.dot(flat_im, a_im, precision=HIGH)  16.4 us
    dot_general x16, matrix products, visibility_pass(): jnp.dot(flat_re, a_im, precision=HIGH)  16.4 us
    dot_general x16, matrix products, visibility_pass(): jnp.dot(flat_re, a_re, precision=HIGH)  16.3 us
  transfers between devices with their start and end apart: 1, of which 1 were waited for; matrix products, arithmetic and copies ran while one was open for 1% of the time, Pallas kernels for 0%

commit v1 on v0

v1 whole, which is shorter than its diff:
```python
import functools
import math

import jax
import jax.numpy as jnp
import numpy as np
from jax import lax
from jax.experimental import pallas as pl
from jax.experimental.pallas import tpu as pltpu
from jax.sharding import PartitionSpec as P

TILE_SIDE = 32
LANES = 128
CHUNK = 512
HIGH = lax.Precision.HIGHEST
MESH = pl.DeviceIdType.MESH
F32 = jnp.float32
BF16 = jnp.bfloat16


def tables():
    side = TILE_SIDE
    index = np.arange(side)
    angle = 2.0 * math.pi / side * (index[:, None] * index[None, :] % side)
    cosine, sine = np.cos(angle) / math.sqrt(side), -np.sin(angle) / math.sqrt(side)
    lane = np.arange(LANES)
    rows = side * side // LANES
    per = LANES // side
    line = np.stack(
        [
            np.concatenate([m[:, per * r + lane // side] for m in (cosine, sine)], axis=0)
            for r in range(rows)
        ]
    )
    fre, fim = cosine[lane % side], sine[lane % side]
    g_re = np.concatenate([fre, -fim], axis=0)
    g_im = np.concatenate([fim, fre], axis=0)
    right = np.concatenate([np.tile(np.concatenate([g_re, -g_im], 1), (1, 4)),
                            np.tile(np.concatenate([g_im, g_re], 1), (1, 4))], axis=1)
    block_re = np.concatenate(
        [cosine, -sine, cosine, -sine, sine, cosine, sine, cosine], axis=0
    )
    block_im = np.concatenate(
        [-sine, -cosine, -sine, -cosine, cosine, -sine, cosine, -sine], axis=0
    )
    back = np.concatenate([np.tile(block_re, (1, per)), np.tile(block_im, (1, per))], axis=1)
    return line.astype(np.float32), right.astype(np.float32), back.astype(np.float32)


def split(values):
    high = values.astype(BF16)
    return high, (values - high.astype(F32)).astype(BF16)


def greet(vis, chan, n_vis, n_chan):
    barrier = pltpu.get_barrier_semaphore()

    def hello(k, carry):
        pl.semaphore_signal(
            barrier, inc=1, device_id=(lax.rem(vis + k, n_vis), chan), device_id_type=MESH
        )
        return carry

    lax.fori_loop(1, n_vis, hello, 0)
    for k in range(1, n_chan):
        pl.semaphore_signal(
            barrier, inc=1, device_id=(vis, lax.rem(chan + k, n_chan)), device_id_type=MESH
        )
    pl.semaphore_wait(barrier, n_vis - 1 + n_chan - 1)


def offset_of(channel, n_chan):
    return (channel.astype(F32) - 0.5 * (n_chan - 1)) / n_chan


def gather_kernel(n_vis, n_chan, model_ref, tiles_ref, send, stage, cs, cr, vs, vr):
    vis, chan = lax.axis_index("vis"), lax.axis_index("chan")
    tile_dev, piece = model_ref.shape[1], model_ref.shape[2]
    per = piece // LANES
    first, second = model_ref[0], model_ref[1]
    for k in range(1, n_chan):
        send[k] = first + offset_of(lax.rem(chan + k, n_chan), n_chan) * second
    stage[chan] = first + offset_of(chan, n_chan) * second
    greet(vis, chan, n_vis, n_chan)
    swaps = []
    for k in range(1, n_chan):
        swap = pltpu.make_async_remote_copy(
            src_ref=send.at[k],
            dst_ref=stage.at[chan],
            send_sem=cs.at[k],
            recv_sem=cr.at[k],
            device_id=(vis, lax.rem(chan + k, n_chan)),
            device_id_type=MESH,
        )
        swap.start()
        swaps.append(swap)
    for swap in swaps:
        swap.wait()
    own = pl.ds(vis * tile_dev, tile_dev)
    for c in range(n_chan):
        part = stage[c]
        for j in range(per):
            tiles_ref[own, c * per + j, :] = part[:, LANES * j : LANES * (j + 1)]

    def copy(k):
        return pltpu.make_async_remote_copy(
            src_ref=tiles_ref.at[own],
            dst_ref=tiles_ref.at[own],
            send_sem=vs.at[k],
            recv_sem=vr.at[k],
            device_id=(lax.rem(vis + k, n_vis), chan),
            device_id_type=MESH,
        )

    def begin(k, carry):
        copy(k).start()
        return carry

    def finish(k, carry):
        copy(k).wait()
        return carry

    lax.fori_loop(1, n_vis, begin, 0)
    lax.fori_loop(1, n_vis, finish, 0)


def return_kernel(n_vis, n_chan, tiles_ref, step_ref, landed, send, stage, cs, cr, vs, vr):
    vis, chan = lax.axis_index("vis"), lax.axis_index("chan")
    tile_dev, piece = step_ref.shape[1], step_ref.shape[2]
    per = piece // LANES
    rows = per * n_chan
    greet(vis, chan, n_vis, n_chan)

    def copy(k):
        other = lax.rem(vis + k, n_vis)
        return pltpu.make_async_remote_copy(
            src_ref=tiles_ref.at[other],
            dst_ref=landed.at[k],
            send_sem=vs.at[k],
            recv_sem=vr.at[k],
            device_id=(other, chan),
            device_id_type=MESH,
        )

    def begin(k, carry):
        copy(k).start()
        return carry

    lax.fori_loop(1, n_vis, begin, 0)

    def added(total, block):
        return tuple(
            total[t] + block[:rows] * block[rows + t : rows + t + 1] for t in range(tile_dev)
        )

    def finish(k, total):
        copy(k).wait()
        return added(total, landed[k])

    zero = jnp.zeros((rows, LANES), F32)
    dirty = lax.fori_loop(1, n_vis, finish, added((zero,) * tile_dev, tiles_ref[vis]))
    for c in range(n_chan):
        for t in range(tile_dev):
            for j in range(per):
                row = c * per + j
                send[c, t : t + 1, LANES * j : LANES * (j + 1)] = dirty[t][row : row + 1]
    stage[chan] = send[chan]
    swaps = []
    for k in range(1, n_chan):
        other = lax.rem(chan + k, n_chan)
        swap = pltpu.make_async_remote_copy(
            src_ref=send.at[other],
            dst_ref=stage.at[chan],
            send_sem=cs.at[k],
            recv_sem=cr.at[k],
            device_id=(vis, other),
            device_id_type=MESH,
        )
        swap.start()
        swaps.append(swap)
    for swap in swaps:
        swap.wait()
    offsets = [(c - 0.5 * (n_chan - 1)) / n_chan for c in range(n_chan)]
    plain, sloped = stage[0], offsets[0] * stage[0]
    for c in range(1, n_chan):
        plain = plain + stage[c]
        sloped = sloped + offsets[c] * stage[c]
    step_ref[0] = plain / n_chan
    step_ref[1] = sloped / sum(x * x for x in offsets)


def block_kernel(
    listed_ref,
    tiles_ref,
    kernels_ref,
    data_ref,
    weight_ref,
    slot_ref,
    wplane_ref,
    offset_ref,
    line_ref,
    right_ref,
    back_ref,
    residual_ref,
    out_ref,
    w_ref,
    g_ref,
    y_ref,
    acc_ref,
):
    side = TILE_SIDE
    slots = listed_ref.shape[2]
    rows = tiles_ref.shape[1]
    tile_dev = tiles_ref.shape[0] // out_ref.shape[0]
    planes, taps = kernels_ref.shape[1], kernels_ref.shape[2]
    count = slot_ref.shape[1]
    size = y_ref.shape[1]

    for s in range(slots):
        tile = tiles_ref[listed_ref[0, 0, s]]
        w = line_ref[0] * tile[0:1]
        for r in range(1, rows):
            w = w + line_ref[r] * tile[r : r + 1]
        w_ref[side * s : side * (s + 1), :LANES] = w[:side]
        w_ref[side * s : side * (s + 1), LANES:] = w[side:]
    half = slots * side
    low_part = lax.broadcasted_iota(jnp.int32, (half, 2 * LANES), 1) >= LANES
    for i in range(2):
        grid = jnp.dot(
            w_ref[...],
            right_ref[:, 2 * LANES * i : 2 * LANES * (i + 1)],
            precision=HIGH,
            preferred_element_type=F32,
        )
        high = grid.astype(BF16).astype(F32)
        g_ref[half * i : half * (i + 1), :] = jnp.where(low_part, grid - high, high).astype(BF16)

    k_high, k_low = split(jnp.concatenate([kernels_ref[0], kernels_ref[1]], axis=1))
    acc_ref[...] = jnp.zeros_like(acc_ref)
    cell = lax.broadcasted_iota(jnp.int32, (side, size), 0)
    plane = lax.broadcasted_iota(jnp.int32, (planes, size), 0)

    def body(step, carry):
        here = pl.ds(pl.multiple_of(step * size, size), size)
        slot = slot_ref[:, here]
        picker = jnp.where(plane == wplane_ref[:, here], 1.0, 0.0).astype(BF16)
        contract = (((0,), (0,)), ((), ()))
        tap = lax.dot_general(
            k_high, picker, contract, preferred_element_type=F32
        ) + lax.dot_general(k_low, picker, contract, preferred_element_type=F32)

        def place(offset):
            shift = cell - offset
            re = jnp.zeros((side, size), F32)
            im = jnp.zeros((side, size), F32)
            for t in range(taps):
                hit = shift == t
                re = jnp.where(hit, tap[t : t + 1], re)
                im = jnp.where(hit, tap[taps + t : taps + t + 1], im)
            return re, im

        a_re, a_im = place(offset_ref[0, :, here])
        b_re, b_im = place(offset_ref[1, :, here])
        b_high, b_low = split(jnp.concatenate([b_re, b_im], axis=0))
        both = jnp.concatenate([b_high, b_low], axis=0)
        y_ref[...] = jnp.dot(
            g_ref[...], jnp.concatenate([both, both], axis=0), preferred_element_type=F32
        )
        s_re = y_ref[:side]
        s_im = y_ref[half : half + side]
        for s in range(1, slots):
            hit = slot == s
            s_re = jnp.where(hit, y_ref[side * s : side * (s + 1)], s_re)
            s_im = jnp.where(hit, y_ref[half + side * s : half + side * (s + 1)], s_im)
        pred_re = jnp.sum(s_re * a_re - s_im * a_im, axis=0, keepdims=True)
        pred_im = jnp.sum(s_re * a_im + s_im * a_re, axis=0, keepdims=True)
        weight = weight_ref[:, here]
        res_re = weight * (data_ref[0, :, here] - pred_re)
        res_im = weight * (data_ref[1, :, here] - pred_im)
        residual_ref[0, :, here] = res_re
        residual_ref[1, :, here] = res_im
        z_high, z_low = split(
            jnp.concatenate(
                [res_re * a_re + res_im * a_im, res_im * a_re - res_re * a_im], axis=0
            )
        )
        z = jnp.concatenate([z_high, z_low], axis=0)
        group, parity = slot // 2, slot % 2
        left = jnp.concatenate(
            [z * jnp.where(group == g, 1.0, 0.0).astype(BF16) for g in range(slots // 2)], axis=0
        )
        right = jnp.concatenate(
            [both * jnp.where(parity == h, 1.0, 0.0).astype(BF16) for h in range(2)], axis=0
        )
        acc_ref[...] += lax.dot_general(
            left, right, (((1,), (1,)), ((), ())), preferred_element_type=F32
        )
        return carry

    lax.fori_loop(0, count // size, body, 0)

    for s in range(slots):
        g, h = s // 2, s % 2
        block = acc_ref[4 * side * g : 4 * side * (g + 1), LANES * h : LANES * (h + 1)]
        block = block[: 2 * side] + block[2 * side :]
        w_ref[side * s : side * (s + 1), :LANES] = block[:side]
        w_ref[side * s : side * (s + 1), LANES:] = block[side:]
    y_ref[:half, : 2 * LANES] = jnp.dot(
        w_ref[...], back_ref[...], precision=HIGH, preferred_element_type=F32
    )
    out_ref[...] = jnp.zeros_like(out_ref)
    marks = lax.broadcasted_iota(jnp.int32, (rows, LANES), 0)
    for s in range(slots):
        listed = listed_ref[0, 0, s]
        owner = listed // tile_dev
        u_re = y_ref[side * s : side * (s + 1), :LANES]
        u_im = y_ref[side * s : side * (s + 1), LANES : 2 * LANES]
        lines = [
            jnp.sum(line_ref[r, :side] * u_re + line_ref[r, side:] * u_im, axis=0, keepdims=True)
            for r in range(rows)
        ]
        out_ref[owner, :rows, :] = jnp.concatenate(lines, axis=0)
        out_ref[owner, rows:, :] = jnp.where(marks == listed % tile_dev, 1.0, 0.0)


VMEM = pl.BlockSpec(memory_space=pltpu.VMEM)
SMEM = pl.BlockSpec(memory_space=pltpu.SMEM)


def block_call(tiles, kernels, vis_data, vis_weight, tile_list, vis_slot, vis_wplane, vis_offset, n_vis):
    line, right, back = tables()
    rows = tiles.shape[1]
    slots = tile_list.shape[2]
    half = slots * TILE_SIDE
    count = vis_slot.shape[1]
    size = min(CHUNK, count)
    return pl.pallas_call(
        block_kernel,
        out_shape=(
            jax.ShapeDtypeStruct(vis_data.shape, F32),
            jax.ShapeDtypeStruct((n_vis, 2 * rows, LANES), F32),
        ),
        in_specs=[SMEM] + [VMEM] * 10,
        out_specs=(VMEM, VMEM),
        scratch_shapes=[
            pltpu.VMEM((half, 2 * LANES), F32),
            pltpu.VMEM((2 * half, 2 * LANES), BF16),
            pltpu.VMEM((2 * half, size), F32),
            pltpu.VMEM((slots // 2 * 4 * TILE_SIDE, 2 * LANES), F32),
        ],
        compiler_params=pltpu.CompilerParams(vmem_limit_bytes=40 * 1024 * 1024),
        name="block",
    )(
        tile_list, tiles, kernels, vis_data, vis_weight, vis_slot, vis_wplane, vis_offset,
        jnp.asarray(line), jnp.asarray(right), jnp.asarray(back),
    )


def shards(model, kernels, vis_data, vis_weight, tile_list, vis_slot, vis_wplane, vis_offset):
    n_vis, n_chan = lax.axis_size("vis"), lax.axis_size("chan")
    tile_dev, piece = model.shape[1], model.shape[2]
    rows = TILE_SIDE * TILE_SIDE // LANES

    def semaphores():
        return [
            pltpu.SemaphoreType.DMA((n_chan,)),
            pltpu.SemaphoreType.DMA((n_chan,)),
            pltpu.SemaphoreType.DMA((n_vis,)),
            pltpu.SemaphoreType.DMA((n_vis,)),
        ]

    pieces = pltpu.VMEM((n_chan, tile_dev, piece), F32)
    tiles = pl.pallas_call(
        functools.partial(gather_kernel, n_vis, n_chan),
        out_shape=jax.ShapeDtypeStruct((n_vis * tile_dev, rows, LANES), F32),
        in_specs=[VMEM],
        out_specs=VMEM,
        scratch_shapes=[pieces, pieces] + semaphores(),
        compiler_params=pltpu.CompilerParams(collective_id=0, has_side_effects=True),
        name="gather",
    )(model)
    residual, dirty = block_call(
        tiles, kernels, vis_data, vis_weight, tile_list, vis_slot, vis_wplane, vis_offset, n_vis
    )
    model_step = pl.pallas_call(
        functools.partial(return_kernel, n_vis, n_chan),
        out_shape=jax.ShapeDtypeStruct(model.shape, F32),
        in_specs=[VMEM],
        out_specs=VMEM,
        scratch_shapes=[pltpu.VMEM((n_vis, 2 * rows, LANES), F32), pieces, pieces] + semaphores(),
        compiler_params=pltpu.CompilerParams(collective_id=1, has_side_effects=True),
        name="back",
    )(dirty)
    return (model_step, residual)


def solution(mesh):
    placed = (
        P(None, "vis", "chan"),
        P(),
        P(None, "chan", "vis"),
        P("chan", "vis"),
        P("chan", "vis", None),
        P("chan", "vis"),
        P("chan", "vis"),
        P(None, "chan", "vis"),
    )
    return jax.shard_map(
        shards,
        mesh=mesh,
        in_specs=placed,
        out_specs=(P(None, "vis", "chan"), P(None, "chan", "vis")),
        check_vma=False,
    )
```

time: 359 us -> 58.4 us (0.16)
  matrix products: 154 us -> 0 us
  waiting for transfers between devices: 100 us -> 0 us
  blocking collectives: 49.6 us -> 0 us
  Pallas kernels: 0 us -> 48.2 us
  other arithmetic: 16.2 us -> 0 us
  between operations: 15 us -> 0.71 us
  local copies, waits for them, and re-layouts: 20.4 us -> 8.92 us
    dot_general x176 -> x0, matrix products: 154 us -> none  [the longest x64 70.7 us: crossed(): lax.dot_general(left, right, (((1,), (1,)), ((), ())), precision=HIGH)]
    unnamed x2 -> x0, waiting for transfers between devices: 100 us -> none
    all_gather x3 -> x0, blocking collectives: 49.6 us -> none  [the longest x1 45.4 us: shards(): piece = lax.all_gather(packed, 'vis', axis=0, tiled=True)]
    pallas_call x0 -> x3, Pallas kernels: none -> 48.2 us  [the longest x1 21.6 us: block_call(): pl.pallas_call(block_kernel, out_shape=(jax.ShapeDtypeStruct(vis_data.sha...]
    add x33 -> x0, other arithmetic: 4.53 us -> none  [the longest x16 2.34 us: one_block(): return ((carry[0] + part_re, carry[1] + part_im), (res_re, res_im))]
    mul x32 -> x0, other arithmetic: 4.49 us -> none  [the longest x16 4.18 us: visibility_pass(): owner[:, None, :] * (res_im * b_re - res_re * b_im)[None]]
    reshape x38 -> x0, local copies, waits for them, and re-layouts: 4.26 us -> none  [the longest x16 1.79 us: visibility_pass(): part_re.reshape(slots, side, side)]
    another operation x40 -> x0, local copies, waits for them, and re-layouts: 3.78 us -> none  [the longest x16 1.82 us: visibility_pass(): flat_re = grid_re.reshape(slots * side, side)]
  transfers between devices with their start and end apart: 1 -> 0, of which waited for: 1 -> 0; matrix products, arithmetic and copies ran while one was open for 1% -> 0% of each run, Pallas kernels for 0% -> 0%
where the time goes in v1:
time: 58.4 us; the launch traced here: 57.8 us
  Pallas kernels  48.2 us (83%)
  local copies, waits for them, and re-layouts  8.92 us (15%)
  between operations  0.71 us (1%)
    pallas_call x1, Pallas kernels, block_call(): pl.pallas_call(block_kernel, out_shape=(jax.ShapeDtypeStruct(vis_data.sha...  21.6 us
    pallas_call x1, Pallas kernels, shards(): pl.pallas_call(functools.partial(gather_kernel, n_vis, n_chan), out_shape...  14.7 us
    pallas_call x1, Pallas kernels, shards(): pl.pallas_call(functools.partial(return_kernel, n_vis, n_chan), out_shape...  12 us
    unnamed x24, local copies, waits for them, and re-layouts  8.92 us

profile of v1, /device:TPU:0, one launch (start us, length us, event | category | flops | bytes accessed | tf_op | source)
XLA Modules:
  0.0 57.8 jit_solution(2937051716403486156)
XLA Ops:
  0.6 0.0 copy-start.2
  0.6 0.8 %copy.13.kernels_ref = f32[2,32,8]{2,1,0:T(8,128)S(1)} copy(f32[2,32,8]{1,2,0:T(8,128)} %param.12) | data formatting | bytes 4096 | tf_op args[1]
  1.5 0.0 copy-start.7
  1.5 0.0 copy-start.10
  1.5 14.7 %gather.1.tiles_ref = f32[64,8,128]{2,1,0:T(8,128)} custom-call(f32[2,4,512]{2,1,0:T(4,128)} %model_ref.1), custom_call_target="tpu_custom_call" | custom-call | tf_op jit(solution)/shard_map/gather/pallas_call | solution.py:373
  16.2 0.0 copy-done.2
  16.2 0.0 copy-done.7
  16.2 0.0 copy-done.10
  16.2 0.0 copy-start
  16.2 0.9 %copy-done = f32[64,8,128]{2,1,0:T(8,128)S(1)} copy-done((f32[64,8,128]{2,1,0:T(8,128)S(1)}, f32[64,8,128]{2,1,0:T(8,128)}, u32[]{:S(2)}) %copy-start) | copy-done | bytes 262168
  17.1 0.0 copy-start.1
  17.1 1.0 %copy-done.1 = f32[256,512]{1,0:T(8,128)S(1)} copy-done((f32[256,512]{1,0:T(8,128)S(1)}, f32[256,512]{1,0:T(8,128)}, u32[]{:S(2)}) %copy-start.1) | copy-done | bytes 524312
  18.2 0.0 copy-start.3
  18.2 0.9 %copy-done.3 = f32[8,64,128]{2,1,0:T(8,128)S(1)} copy-done((f32[8,64,128]{2,1,0:T(8,128)S(1)}, f32[8,64,128]{2,1,0:T(8,128)}, u32[]{:S(2)}) %copy-start.3) | copy-done | bytes 262168
  19.1 0.0 copy-start.5
  19.1 0.8 %copy-done.5 = f32[2,1,8192]{2,1,0:T(1,128)S(1)} copy-done((f32[2,1,8192]{2,1,0:T(1,128)S(1)}, f32[2,1,8192]{2,1,0:T(1,128)}, u32[]{:S(2)}) %copy-start.5) | copy-done | bytes 65560
  20.0 0.0 copy-start.6
  20.0 0.8 %copy-done.6 = s32[2,1,8192]{2,1,0:T(1,128)S(1)} copy-done((s32[2,1,8192]{2,1,0:T(1,128)S(1)}, s32[2,1,8192]{2,1,0:T(1,128)}, u32[]{:S(2)}) %copy-start.6) | copy-done | bytes 65560
  20.8 0.0 copy-start.8
  20.8 0.8 %copy-done.8 = s32[1,8192]{1,0:T(1,128)S(1)} copy-done((s32[1,8192]{1,0:T(1,128)S(1)}, s32[1,8192]{1,0:T(1,128)}, u32[]{:S(2)}) %copy-start.8) | copy-done | bytes 32792
  21.6 0.0 copy-start.9
  21.6 0.8 %copy-done.9 = s32[1,8192]{1,0:T(1,128)S(1)} copy-done((s32[1,8192]{1,0:T(1,128)S(1)}, s32[1,8192]{1,0:T(1,128)}, u32[]{:S(2)}) %copy-start.9) | copy-done | bytes 32792
  22.3 21.6 %block.1 = (f32[2,1,8192]{2,1,0:T(1,128)}, f32[16,16,128]{2,1,0:T(8,128)S(1)}) custom-call(s32[1,1,16]{2,1,0:T(1,128)S(1)} %copy-done.10, f32[64,8,128]{2,1,0:T(8,128)S(1)} %copy-done, f32[2,32,8]{2,1,0:T(8,128)S(1)} %copy.13.kernels_ref, f32[2,1,8192]{2,1,0:T(1,128)S(1)} %copy-done.5, f32[1,8192]{1,0:T(1,128)S(1)} %copy-done.7, s32[1,8192]{1,0:T(1,128)S(1)} %copy-done.8, ...), custom_call_target="tpu_custom_call" | custom-call | tf_op jit(solution)/shard_map/block/pallas_call | solution.py:337
  43.9 0.0 copy-start.4
  43.9 0.6 %copy-done.4 = f32[16,16,128]{2,1,0:T(8,128)} copy-done((f32[16,16,128]{2,1,0:T(8,128)}, f32[16,16,128]{2,1,0:T(8,128)S(1)}, u32[]{:S(2)}) %copy-start.4) | copy-done | bytes 131096
  44.5 12.0 %back.1 = f32[2,4,512]{2,1,0:T(4,128)} custom-call(f32[16,16,128]{2,1,0:T(8,128)} %copy-done.4), custom_call_target="tpu_custom_call" | custom-call | tf_op jit(solution)/shard_map/back/pallas_call | solution.py:385
  56.5 1.3 %copy.15 = f32[2,4,512]{2,1,0:T(4,128)} copy(f32[2,4,512]{2,1,0:T(4,128)} %back.1) | data formatting | bytes 32768
Async XLA Ops:
  0.6 15.5 %copy-start.2 = (f32[256,256]{1,0:T(8,128)S(1)}, f32[256,256]{1,0:T(8,128)}, u32[]{:S(2)}) copy-start(f32[256,256]{1,0:T(8,128)} %constant.8.clone.back_ref) | copy-start | bytes 786436
  1.5 14.7 %copy-start.7 = (f32[1,8192]{1,0:T(1,128)S(1)}, f32[1,8192]{1,0:T(1,128)}, u32[]{:S(2)}) copy-start(f32[1,8192]{1,0:T(1,128)} %weight_ref.1) | copy-start | bytes 98308
  1.5 14.7 %copy-start.10 = (s32[1,1,16]{2,1,0:T(1,128)S(1)}, s32[1,1,16]{2,1,0:T(1,128)}, u32[]{:S(2)}) copy-start(s32[1,1,16]{2,1,0:T(1,128)} %listed_ref.1) | copy-start | bytes 196
  16.2 1.0 %copy-start = (f32[64,8,128]{2,1,0:T(8,128)S(1)}, f32[64,8,128]{2,1,0:T(8,128)}, u32[]{:S(2)}) copy-start(f32[64,8,128]{2,1,0:T(8,128)} %gather.1.tiles_ref) | copy-start | bytes 786436
  17.1 1.0 %copy-start.1 = (f32[256,512]{1,0:T(8,128)S(1)}, f32[256,512]{1,0:T(8,128)}, u32[]{:S(2)}) copy-start(f32[256,512]{1,0:T(8,128)} %constant.7.clone.right_ref) | copy-start | bytes 1572868
  18.2 0.9 %copy-start.3 = (f32[8,64,128]{2,1,0:T(8,128)S(1)}, f32[8,64,128]{2,1,0:T(8,128)}, u32[]{:S(2)}) copy-start(f32[8,64,128]{2,1,0:T(8,128)} %constant.6.clone.line_ref) | copy-start | bytes 786436
  19.1 0.8 %copy-start.5 = (f32[2,1,8192]{2,1,0:T(1,128)S(1)}, f32[2,1,8192]{2,1,0:T(1,128)}, u32[]{:S(2)}) copy-start(f32[2,1,8192]{2,1,0:T(1,128)} %data_ref.1) | copy-start | bytes 196612
  20.0 0.8 %copy-start.6 = (s32[2,1,8192]{2,1,0:T(1,128)S(1)}, s32[2,1,8192]{2,1,0:T(1,128)}, u32[]{:S(2)}) copy-start(s32[2,1,8192]{2,1,0:T(1,128)} %offset_ref.1) | copy-start | bytes 196612
  20.8 0.8 %copy-start.8 = (s32[1,8192]{1,0:T(1,128)S(1)}, s32[1,8192]{1,0:T(1,128)}, u32[]{:S(2)}) copy-start(s32[1,8192]{1,0:T(1,128)} %slot_ref.1) | copy-start | bytes 98308
  21.6 0.8 %copy-start.9 = (s32[1,8192]{1,0:T(1,128)S(1)}, s32[1,8192]{1,0:T(1,128)}, u32[]{:S(2)}) copy-start(s32[1,8192]{1,0:T(1,128)} %wplane_ref.1) | copy-start | bytes 98308
  43.9 0.6 %copy-start.4 = (f32[16,16,128]{2,1,0:T(8,128)}, f32[16,16,128]{2,1,0:T(8,128)S(1)}, u32[]{:S(2)}) copy-start(f32[16,16,128]{2,1,0:T(8,128)S(1)} %get-tuple-element.4.tiles_ref) | copy-start | bytes 393220

commit v2 on v1

--- a/solution.py
+++ b/solution.py
@@ -12,6 +12,7 @@
 TILE_SIDE = 32
 LANES = 128
 CHUNK = 512
+PARTS = 2
 HIGH = lax.Precision.HIGHEST
 MESH = pl.DeviceIdType.MESH
 F32 = jnp.float32
@@ -124,9 +125,9 @@
     lax.fori_loop(1, n_vis, finish, 0)
 
 
-def return_kernel(n_vis, n_chan, tiles_ref, step_ref, landed, send, stage, cs, cr, vs, vr):
+def return_kernel(n_vis, n_chan, tiles_ref, stage, landed, send, cs, cr, vs, vr):
     vis, chan = lax.axis_index("vis"), lax.axis_index("chan")
-    tile_dev, piece = step_ref.shape[1], step_ref.shape[2]
+    tile_dev, piece = stage.shape[1], stage.shape[2]
     per = piece // LANES
     rows = per * n_chan
     greet(vis, chan, n_vis, n_chan)
@@ -180,42 +181,34 @@
         swaps.append(swap)
     for swap in swaps:
         swap.wait()
-    offsets = [(c - 0.5 * (n_chan - 1)) / n_chan for c in range(n_chan)]
-    plain, sloped = stage[0], offsets[0] * stage[0]
-    for c in range(1, n_chan):
-        plain = plain + stage[c]
-        sloped = sloped + offsets[c] * stage[c]
-    step_ref[0] = plain / n_chan
-    step_ref[1] = sloped / sum(x * x for x in offsets)
 
 
 def block_kernel(
     listed_ref,
     tiles_ref,
     kernels_ref,
-    data_ref,
-    weight_ref,
-    slot_ref,
-    wplane_ref,
-    offset_ref,
-    line_ref,
-    right_ref,
-    back_ref,
-    residual_ref,
-    out_ref,
-    w_ref,
-    g_ref,
-    y_ref,
-    acc_ref,
+    *rest,
 ):
+    sources, rest = rest[:8], rest[8:]
+    residual_ref, out_ref, w_ref, g_ref, y_ref, acc_ref, z_ref, b_ref = rest[:8]
+    held, sems = rest[8:16], rest[16]
+    fetches = [
+        pltpu.make_async_copy(source, target, sems.at[i])
+        for i, (source, target) in enumerate(zip(sources, held))
+    ]
+    for fetch in fetches:
+        fetch.start()
+    line_ref, right_ref, data_ref, weight_ref, slot_ref, wplane_ref, offset_ref, back_ref = held
     side = TILE_SIDE
     slots = listed_ref.shape[2]
     rows = tiles_ref.shape[1]
     tile_dev = tiles_ref.shape[0] // out_ref.shape[0]
     planes, taps = kernels_ref.shape[1], kernels_ref.shape[2]
     count = slot_ref.shape[1]
-    size = y_ref.shape[1]
-
+    size = y_ref.shape[2]
+
+    fetches[0].wait()
+    fetches[1].wait()
     for s in range(slots):
         tile = tiles_ref[listed_ref[0, 0, s]]
         w = line_ref[0] * tile[0:1]
@@ -237,11 +230,21 @@
 
     k_high, k_low = split(jnp.concatenate([kernels_ref[0], kernels_ref[1]], axis=1))
     acc_ref[...] = jnp.zeros_like(acc_ref)
+    z_ref[...] = jnp.zeros_like(z_ref)
+    b_ref[...] = jnp.zeros_like(b_ref)
+    for fetch in fetches[2:]:
+        fetch.wait()
     cell = lax.broadcasted_iota(jnp.int32, (side, size), 0)
     plane = lax.broadcasted_iota(jnp.int32, (planes, size), 0)
 
-    def body(step, carry):
-        here = pl.ds(pl.multiple_of(step * size, size), size)
+    def grid_held():
+        acc_ref[...] += lax.dot_general(
+            z_ref[...], b_ref[...], (((1,), (1,)), ((), ())), preferred_element_type=F32
+        )
+
+    def part(step, i):
+        here = pl.ds(pl.multiple_of(step * (PARTS * size) + i * size, size), size)
+        y = y_ref.at[i]
         slot = slot_ref[:, here]
         picker = jnp.where(plane == wplane_ref[:, here], 1.0, 0.0).astype(BF16)
         contract = (((0,), (0,)), ((), ()))
@@ -263,15 +266,15 @@
         b_re, b_im = place(offset_ref[1, :, here])
         b_high, b_low = split(jnp.concatenate([b_re, b_im], axis=0))
         both = jnp.concatenate([b_high, b_low], axis=0)
-        y_ref[...] = jnp.dot(
+        y[...] = jnp.dot(
             g_ref[...], jnp.concatenate([both, both], axis=0), preferred_element_type=F32
         )
-        s_re = y_ref[:side]
-        s_im = y_ref[half : half + side]
+        s_re = y[:side]
+        s_im = y[half : half + side]
         for s in range(1, slots):
             hit = slot == s
-            s_re = jnp.where(hit, y_ref[side * s : side * (s + 1)], s_re)
-            s_im = jnp.where(hit, y_ref[half + side * s : half + side * (s + 1)], s_im)
+            s_re = jnp.where(hit, y[side * s : side * (s + 1)], s_re)
+            s_im = jnp.where(hit, y[half + side * s : half + side * (s + 1)], s_im)
         pred_re = jnp.sum(s_re * a_re - s_im * a_im, axis=0, keepdims=True)
         pred_im = jnp.sum(s_re * a_im + s_im * a_re, axis=0, keepdims=True)
         weight = weight_ref[:, here]
@@ -292,12 +295,18 @@
         right = jnp.concatenate(
             [both * jnp.where(parity == h, 1.0, 0.0).astype(BF16) for h in range(2)], axis=0
         )
-        acc_ref[...] += lax.dot_general(
-            left, right, (((1,), (1,)), ((), ())), preferred_element_type=F32
-        )
+        return left, right
+
+    def body(step, carry):
+        grid_held()
+        made = [part(step, i) for i in range(PARTS)]
+        for i, (left, right) in enumerate(made):
+            z_ref[:, size * i : size * (i + 1)] = left
+            b_ref[:, size * i : size * (i + 1)] = right
         return carry
 
-    lax.fori_loop(0, count // size, body, 0)
+    lax.fori_loop(0, count // (PARTS * size), body, 0)
+    grid_held()
 
     for s in range(slots):
         g, h = s // 2, s % 2
@@ -305,7 +314,7 @@
         block = block[: 2 * side] + block[2 * side :]
         w_ref[side * s : side * (s + 1), :LANES] = block[:side]
         w_ref[side * s : side * (s + 1), LANES:] = block[side:]
-    y_ref[:half, : 2 * LANES] = jnp.dot(
+    y_ref[0, :half, : 2 * LANES] = jnp.dot(
         w_ref[...], back_ref[...], precision=HIGH, preferred_element_type=F32
     )
     out_ref[...] = jnp.zeros_like(out_ref)
@@ -313,8 +322,8 @@
     for s in range(slots):
         listed = listed_ref[0, 0, s]
         owner = listed // tile_dev
-        u_re = y_ref[side * s : side * (s + 1), :LANES]
-        u_im = y_ref[side * s : side * (s + 1), LANES : 2 * LANES]
+        u_re = y_ref[0, side * s : side * (s + 1), :LANES]
+        u_im = y_ref[0, side * s : side * (s + 1), LANES : 2 * LANES]
         lines = [
             jnp.sum(line_ref[r, :side] * u_re + line_ref[r, side:] * u_im, axis=0, keepdims=True)
             for r in range(rows)
@@ -333,26 +342,31 @@
     slots = tile_list.shape[2]
     half = slots * TILE_SIDE
     count = vis_slot.shape[1]
-    size = min(CHUNK, count)
+    size = CHUNK
+    moved = (line, right, vis_data, vis_weight, vis_slot, vis_wplane, vis_offset, back)
+    moved = tuple(jnp.asarray(array) for array in moved)
     return pl.pallas_call(
         block_kernel,
         out_shape=(
             jax.ShapeDtypeStruct(vis_data.shape, F32),
             jax.ShapeDtypeStruct((n_vis, 2 * rows, LANES), F32),
         ),
-        in_specs=[SMEM] + [VMEM] * 10,
+        in_specs=[SMEM, VMEM, VMEM] + [pl.BlockSpec(memory_space=pltpu.HBM)] * len(moved),
         out_specs=(VMEM, VMEM),
         scratch_shapes=[
             pltpu.VMEM((half, 2 * LANES), F32),
             pltpu.VMEM((2 * half, 2 * LANES), BF16),
-            pltpu.VMEM((2 * half, size), F32),
+            pltpu.VMEM((PARTS, 2 * half, size), F32),
             pltpu.VMEM((slots // 2 * 4 * TILE_SIDE, 2 * LANES), F32),
-        ],
+            pltpu.VMEM((slots // 2 * 4 * TILE_SIDE, PARTS * size), BF16),
+            pltpu.VMEM((2 * LANES, PARTS * size), BF16),
+        ]
+        + [pltpu.VMEM(array.shape, array.dtype) for array in moved]
+        + [pltpu.SemaphoreType.DMA((len(moved),))],
         compiler_params=pltpu.CompilerParams(vmem_limit_bytes=40 * 1024 * 1024),
         name="block",
     )(
-        tile_list, tiles, kernels, vis_data, vis_weight, vis_slot, vis_wplane, vis_offset,
-        jnp.asarray(line), jnp.asarray(right), jnp.asarray(back),
+        tile_list, tiles, kernels, *moved
     )
 
 
@@ -382,16 +396,19 @@
     residual, dirty = block_call(
         tiles, kernels, vis_data, vis_weight, tile_list, vis_slot, vis_wplane, vis_offset, n_vis
     )
-    model_step = pl.pallas_call(
+    every = pl.pallas_call(
         functools.partial(return_kernel, n_vis, n_chan),
-        out_shape=jax.ShapeDtypeStruct(model.shape, F32),
+        out_shape=jax.ShapeDtypeStruct((n_chan, tile_dev, piece), F32),
         in_specs=[VMEM],
         out_specs=VMEM,
-        scratch_shapes=[pltpu.VMEM((n_vis, 2 * rows, LANES), F32), pieces, pieces] + semaphores(),
+        scratch_shapes=[pltpu.VMEM((n_vis, 2 * rows, LANES), F32), pieces] + semaphores(),
         compiler_params=pltpu.CompilerParams(collective_id=1, has_side_effects=True),
         name="back",
     )(dirty)
-    return (model_step, residual)
+    offsets = [(c - 0.5 * (n_chan - 1)) / n_chan for c in range(n_chan)]
+    plain = sum(every[c] for c in range(n_chan)) / n_chan
+    sloped = sum(offsets[c] * every[c] for c in range(n_chan)) / sum(x * x for x in offsets)
+    return (jnp.stack([plain, sloped]), residual)
 
 
 def solution(mesh):

time: 58.4 us -> 57.7 us (0.988)
  other arithmetic: 0 us -> 1.33 us
  local copies, waits for them, and re-layouts: 8.92 us -> 7.6 us
  Pallas kernels: 48.2 us -> 47.5 us
    unnamed x24 -> x23, local copies, waits for them, and re-layouts: 8.92 us -> 7.6 us
    div x0 -> x1, other arithmetic: none -> 0.72 us  [shards(): plain = sum((every[c] for c in range(n_chan))) / n_chan]
    pallas_call x1, Pallas kernels: 21.6 us -> 20.9 us  [block_call(): pl.pallas_call(block_kernel, out_shape=(jax.ShapeDtypeStruct(vis_data.sha...]
    another operation x0 -> x1, other arithmetic: none -> 0.61 us  [shards(): return (jnp.stack([plain, sloped]), residual)]
where the time goes in v2:
time: 57.7 us; the launch traced here: 57.2 us
  Pallas kernels  47.5 us (82%)
  local copies, waits for them, and re-layouts  7.6 us (13%)
  other arithmetic  1.33 us (2%)
  between operations  0.72 us (1%)
    pallas_call x1, Pallas kernels, block_call(): pl.pallas_call(block_kernel, out_shape=(jax.ShapeDtypeStruct(vis_data.sha...  20.9 us
    pallas_call x1, Pallas kernels, shards(): pl.pallas_call(functools.partial(gather_kernel, n_vis, n_chan), out_shape...  14.7 us
    pallas_call x1, Pallas kernels, shards(): pl.pallas_call(functools.partial(return_kernel, n_vis, n_chan), out_shape...  12 us
    unnamed x23, local copies, waits for them, and re-layouts  7.6 us

profile of v2, /device:TPU:0, one launch (start us, length us, event | category | flops | bytes accessed | tf_op | source)
XLA Modules:
  0.0 57.2 jit_solution(9779975055706790004)
XLA Ops:
  0.6 0.0 copy-start.2
  0.6 0.8 %copy.13.kernels_ref = f32[2,32,8]{2,1,0:T(8,128)S(1)} copy(f32[2,32,8]{1,2,0:T(8,128)} %param.12) | data formatting | bytes 4096 | tf_op args[1]
  1.5 0.0 copy-start.7
  1.5 0.0 copy-start.10
  1.5 14.7 %gather.1.tiles_ref = f32[64,8,128]{2,1,0:T(8,128)} custom-call(f32[2,4,512]{2,1,0:T(4,128)} %model_ref.1), custom_call_target="tpu_custom_call" | custom-call | tf_op jit(solution)/shard_map/gather/pallas_call | solution.py:387
  16.1 0.0 copy-done.2
  16.2 0.0 copy-done.7
  16.2 0.0 copy-done.10
  16.2 0.0 copy-start
  16.2 0.9 %copy-done = f32[64,8,128]{2,1,0:T(8,128)S(1)} copy-done((f32[64,8,128]{2,1,0:T(8,128)S(1)}, f32[64,8,128]{2,1,0:T(8,128)}, u32[]{:S(2)}) %copy-start) | copy-done | bytes 262168
  17.1 0.0 copy-start.1
  17.1 1.0 %copy-done.1 = f32[256,512]{1,0:T(8,128)S(1)} copy-done((f32[256,512]{1,0:T(8,128)S(1)}, f32[256,512]{1,0:T(8,128)}, u32[]{:S(2)}) %copy-start.1) | copy-done | bytes 524312
  18.2 0.0 copy-start.3
  18.2 0.9 %copy-done.3 = f32[8,64,128]{2,1,0:T(8,128)S(1)} copy-done((f32[8,64,128]{2,1,0:T(8,128)S(1)}, f32[8,64,128]{2,1,0:T(8,128)}, u32[]{:S(2)}) %copy-start.3) | copy-done | bytes 262168
  19.1 0.0 copy-start.5
  19.1 0.8 %copy-done.5 = f32[2,1,8192]{2,1,0:T(1,128)S(1)} copy-done((f32[2,1,8192]{2,1,0:T(1,128)S(1)}, f32[2,1,8192]{2,1,0:T(1,128)}, u32[]{:S(2)}) %copy-start.5) | copy-done | bytes 65560
  20.0 0.0 copy-start.6
  20.0 0.8 %copy-done.6 = s32[2,1,8192]{2,1,0:T(1,128)S(1)} copy-done((s32[2,1,8192]{2,1,0:T(1,128)S(1)}, s32[2,1,8192]{2,1,0:T(1,128)}, u32[]{:S(2)}) %copy-start.6) | copy-done | bytes 65560
  20.8 0.0 copy-start.8
  20.8 0.8 %copy-done.8 = s32[1,8192]{1,0:T(1,128)S(1)} copy-done((s32[1,8192]{1,0:T(1,128)S(1)}, s32[1,8192]{1,0:T(1,128)}, u32[]{:S(2)}) %copy-start.8) | copy-done | bytes 32792
  21.6 0.0 copy-start.9
  21.6 0.8 %copy-done.9 = s32[1,8192]{1,0:T(1,128)S(1)} copy-done((s32[1,8192]{1,0:T(1,128)S(1)}, s32[1,8192]{1,0:T(1,128)}, u32[]{:S(2)}) %copy-start.9) | copy-done | bytes 32792
  22.3 20.9 %block.1 = (f32[2,1,8192]{2,1,0:T(1,128)}, f32[16,16,128]{2,1,0:T(8,128)S(1)}) custom-call(s32[1,1,16]{2,1,0:T(1,128)S(1)} %copy-done.10, f32[64,8,128]{2,1,0:T(8,128)S(1)} %copy-done, f32[2,32,8]{2,1,0:T(8,128)S(1)} %copy.13.kernels_ref, f32[8,64,128]{2,1,0:T(8,128)S(1)} %copy-done.3, f32[256,512]{1,0:T(8,128)S(1)} %copy-done.1, ...), custom_call_target="tpu_custom_call" | custom-call | tf_op jit(solution)/shard_map/block/pallas_call | solution.py:348
  43.2 0.0 copy-start.4
  43.2 0.6 %copy-done.4 = f32[16,16,128]{2,1,0:T(8,128)} copy-done((f32[16,16,128]{2,1,0:T(8,128)}, f32[16,16,128]{2,1,0:T(8,128)S(1)}, u32[]{:S(2)}) %copy-start.4) | copy-done | bytes 131096
  43.8 12.0 %back.1 = f32[2,4,512]{2,1,0:T(4,128)} custom-call(f32[16,16,128]{2,1,0:T(8,128)} %copy-done.4), custom_call_target="tpu_custom_call" | custom-call | tf_op jit(solution)/shard_map/back/pallas_call | solution.py:399
  55.8 0.7 %add_multiply_fusion.1 = (f32[1,4,512]{2,1,0:T(4,128)S(1)}, f32[1,4,512]{2,1,0:T(4,128)S(1)}) fusion(f32[2,4,512]{2,1,0:T(4,128)} %back.1), kind=kLoop, calls=%fused_computation.2 | loop fusion | flops 12288 | bytes 32768 | tf_op jit(solution)/shard_map/div | solution.py:409
  56.6 0.6 %pad_maximum_fusion = f32[2,4,512]{2,1,0:T(4,128)} fusion(f32[1,4,512]{2,1,0:T(4,128)S(1)} %get-tuple-element.7, f32[1,4,512]{2,1,0:T(4,128)S(1)} %get-tuple-element.6), kind=kLoop, calls=%fused_computation | loop fusion | flops 4096 | bytes 32768 | tf_op jit(solution)/shard_map/stack | solution.py:411
Async XLA Ops:
  0.6 15.5 %copy-start.2 = (f32[256,256]{1,0:T(8,128)S(1)}, f32[256,256]{1,0:T(8,128)}, u32[]{:S(2)}) copy-start(f32[256,256]{1,0:T(8,128)} %constant.18.clone.rest_7_) | copy-start | bytes 786436
  1.5 14.7 %copy-start.7 = (f32[1,8192]{1,0:T(1,128)S(1)}, f32[1,8192]{1,0:T(1,128)}, u32[]{:S(2)}) copy-start(f32[1,8192]{1,0:T(1,128)} %rest_3_.1) | copy-start | bytes 98308
  1.5 14.7 %copy-start.10 = (s32[1,1,16]{2,1,0:T(1,128)S(1)}, s32[1,1,16]{2,1,0:T(1,128)}, u32[]{:S(2)}) copy-start(s32[1,1,16]{2,1,0:T(1,128)} %listed_ref.1) | copy-start | bytes 196
  16.2 1.0 %copy-start = (f32[64,8,128]{2,1,0:T(8,128)S(1)}, f32[64,8,128]{2,1,0:T(8,128)}, u32[]{:S(2)}) copy-start(f32[64,8,128]{2,1,0:T(8,128)} %gather.1.tiles_ref) | copy-start | bytes 786436
  17.1 1.0 %copy-start.1 = (f32[256,512]{1,0:T(8,128)S(1)}, f32[256,512]{1,0:T(8,128)}, u32[]{:S(2)}) copy-start(f32[256,512]{1,0:T(8,128)} %constant.17.clone.rest_1_) | copy-start | bytes 1572868
  18.2 0.9 %copy-start.3 = (f32[8,64,128]{2,1,0:T(8,128)S(1)}, f32[8,64,128]{2,1,0:T(8,128)}, u32[]{:S(2)}) copy-start(f32[8,64,128]{2,1,0:T(8,128)} %constant.16.clone.rest_0_) | copy-start | bytes 786436
  19.1 0.8 %copy-start.5 = (f32[2,1,8192]{2,1,0:T(1,128)S(1)}, f32[2,1,8192]{2,1,0:T(1,128)}, u32[]{:S(2)}) copy-start(f32[2,1,8192]{2,1,0:T(1,128)} %rest_2_.1) | copy-start | bytes 196612
  20.0 0.8 %copy-start.6 = (s32[2,1,8192]{2,1,0:T(1,128)S(1)}, s32[2,1,8192]{2,1,0:T(1,128)}, u32[]{:S(2)}) copy-start(s32[2,1,8192]{2,1,0:T(1,128)} %rest_6_.1) | copy-start | bytes 196612
  20.8 0.8 %copy-start.8 = (s32[1,8192]{1,0:T(1,128)S(1)}, s32[1,8192]{1,0:T(1,128)}, u32[]{:S(2)}) copy-start(s32[1,8192]{1,0:T(1,128)} %rest_4_.1) | copy-start | bytes 98308
  21.6 0.8 %copy-start.9 = (s32[1,8192]{1,0:T(1,128)S(1)}, s32[1,8192]{1,0:T(1,128)}, u32[]{:S(2)}) copy-start(s32[1,8192]{1,0:T(1,128)} %rest_5_.1) | copy-start | bytes 98308
  43.2 0.7 %copy-start.4 = (f32[16,16,128]{2,1,0:T(8,128)}, f32[16,16,128]{2,1,0:T(8,128)S(1)}, u32[]{:S(2)}) copy-start(f32[16,16,128]{2,1,0:T(8,128)S(1)} %get-tuple-element.4.tiles_ref) | copy-start | bytes 393220

commit v3 on v2

--- a/solution.py
+++ b/solution.py
@@ -363,7 +363,7 @@
         ]
         + [pltpu.VMEM(array.shape, array.dtype) for array in moved]
         + [pltpu.SemaphoreType.DMA((len(moved),))],
-        compiler_params=pltpu.CompilerParams(vmem_limit_bytes=40 * 1024 * 1024),
+        compiler_params=pltpu.CompilerParams(vmem_limit_bytes=63 * 1024 * 1024),
         name="block",
     )(
         tile_list, tiles, kernels, *moved

time: 57.7 us -> 52.6 us (0.912)
  local copies, waits for them, and re-layouts: 7.6 us -> 1.38 us
  Pallas kernels: 47.5 us -> 48.9 us
    unnamed x23 -> x1, local copies, waits for them, and re-layouts: 7.6 us -> 1.38 us
    pallas_call x1, Pallas kernels: 20.9 us -> 22.3 us  [block_call(): pl.pallas_call(block_kernel, out_shape=(jax.ShapeDtypeStruct(vis_data.sha...]
where the time goes in v3:
time: 52.6 us; the launch traced here: 52.2 us
  Pallas kernels  48.9 us (93%)
  local copies, waits for them, and re-layouts  1.38 us (3%)
  other arithmetic  1.33 us (3%)
  between operations  0.65 us (1%)
    pallas_call x1, Pallas kernels, block_call(): pl.pallas_call(block_kernel, out_shape=(jax.ShapeDtypeStruct(vis_data.sha...  22.3 us
    pallas_call x1, Pallas kernels, shards(): pl.pallas_call(functools.partial(gather_kernel, n_vis, n_chan), out_shape...  14.6 us
    pallas_call x1, Pallas kernels, shards(): pl.pallas_call(functools.partial(return_kernel, n_vis, n_chan), out_shape...  12 us
    unnamed x1, local copies, waits for them, and re-layouts  1.38 us

profile of v3, /device:TPU:0, one launch (start us, length us, event | category | flops | bytes accessed | tf_op | source)
XLA Modules:
  0.0 52.2 jit_solution(13468411470987279908)
XLA Ops:
  0.6 1.4 %copy.13.kernels_ref = f32[2,32,8]{2,1,0:T(8,128)} copy(f32[2,32,8]{1,2,0:T(8,128)} %param.12) | data formatting | bytes 4096 | tf_op args[1]
  2.0 14.6 %gather.1.tiles_ref = f32[64,8,128]{2,1,0:T(8,128)} custom-call(f32[2,4,512]{2,1,0:T(4,128)} %model_ref.1), custom_call_target="tpu_custom_call" | custom-call | tf_op jit(solution)/shard_map/gather/pallas_call | solution.py:387
  16.6 22.3 %block.1 = (f32[2,1,8192]{2,1,0:T(1,128)}, f32[16,16,128]{2,1,0:T(8,128)}) custom-call(s32[1,1,16]{2,1,0:T(1,128)} %listed_ref.1, f32[64,8,128]{2,1,0:T(8,128)} %gather.1.tiles_ref, f32[2,32,8]{2,1,0:T(8,128)} %copy.13.kernels_ref, f32[8,64,128]{2,1,0:T(8,128)} %constant.16.clone.rest_0_, f32[256,512]{1,0:T(8,128)} %constant.17.clone.rest_1_, ...), custom_call_target="tpu_custom_call" | custom-call | tf_op jit(solution)/shard_map/block/pallas_call | solution.py:348
  38.9 12.0 %back.1 = f32[2,4,512]{2,1,0:T(4,128)} custom-call(f32[16,16,128]{2,1,0:T(8,128)} %get-tuple-element.4.tiles_ref), custom_call_target="tpu_custom_call" | custom-call | tf_op jit(solution)/shard_map/back/pallas_call | solution.py:399
  50.9 0.7 %add_multiply_fusion.1 = (f32[1,4,512]{2,1,0:T(4,128)S(1)}, f32[1,4,512]{2,1,0:T(4,128)S(1)}) fusion(f32[2,4,512]{2,1,0:T(4,128)} %back.1), kind=kLoop, calls=%fused_computation.2 | loop fusion | flops 12288 | bytes 32768 | tf_op jit(solution)/shard_map/div | solution.py:409
  51.6 0.6 %pad_maximum_fusion = f32[2,4,512]{2,1,0:T(4,128)} fusion(f32[1,4,512]{2,1,0:T(4,128)S(1)} %get-tuple-element.7, f32[1,4,512]{2,1,0:T(4,128)S(1)} %get-tuple-element.6), kind=kLoop, calls=%fused_computation | loop fusion | flops 4096 | bytes 32768 | tf_op jit(solution)/shard_map/stack | solution.py:411

commit v4 on v3

--- a/solution.py
+++ b/solution.py
@@ -230,8 +230,6 @@
 
     k_high, k_low = split(jnp.concatenate([kernels_ref[0], kernels_ref[1]], axis=1))
     acc_ref[...] = jnp.zeros_like(acc_ref)
-    z_ref[...] = jnp.zeros_like(z_ref)
-    b_ref[...] = jnp.zeros_like(b_ref)
     for fetch in fetches[2:]:
         fetch.wait()
     cell = lax.broadcasted_iota(jnp.int32, (side, size), 0)
@@ -297,15 +295,20 @@
         )
         return left, right
 
-    def body(step, carry):
-        grid_held()
+    def hold(step):
         made = [part(step, i) for i in range(PARTS)]
         for i, (left, right) in enumerate(made):
             z_ref[:, size * i : size * (i + 1)] = left
             b_ref[:, size * i : size * (i + 1)] = right
+
+    def body(step, carry):
+        grid_held()
+        hold(step)
         return carry
 
-    lax.fori_loop(0, count // (PARTS * size), body, 0)
+    hold(0)
+
+    lax.fori_loop(1, count // (PARTS * size), body, 0)
     grid_held()
 
     for s in range(slots):

time: 52.6 us -> 52 us (0.989)
  Pallas kernels: 48.9 us -> 48.3 us
    pallas_call x1, Pallas kernels: 22.3 us -> 21.6 us  [block_call(): pl.pallas_call(block_kernel, out_shape=(jax.ShapeDtypeStruct(vis_data.sha...]
where the time goes in v4:
time: 52 us; the launch traced here: 51.6 us
  Pallas kernels  48.3 us (93%)
  local copies, waits for them, and re-layouts  1.38 us (3%)
  other arithmetic  1.33 us (3%)
  between operations  0.65 us (1%)
    pallas_call x1, Pallas kernels, block_call(): pl.pallas_call(block_kernel, out_shape=(jax.ShapeDtypeStruct(vis_data.sha...  21.6 us
    pallas_call x1, Pallas kernels, shards(): pl.pallas_call(functools.partial(gather_kernel, n_vis, n_chan), out_shape...  14.6 us
    pallas_call x1, Pallas kernels, shards(): pl.pallas_call(functools.partial(return_kernel, n_vis, n_chan), out_shape...  12 us
    unnamed x1, local copies, waits for them, and re-layouts  1.38 us

profile of v4, /device:TPU:0, one launch (start us, length us, event | category | flops | bytes accessed | tf_op | source)
XLA Modules:
  0.0 51.6 jit_solution(5602734659334808451)
XLA Ops:
  0.6 1.4 %copy.13.kernels_ref = f32[2,32,8]{2,1,0:T(8,128)} copy(f32[2,32,8]{1,2,0:T(8,128)} %param.12) | data formatting | bytes 4096 | tf_op args[1]
  2.0 14.6 %gather.1.tiles_ref = f32[64,8,128]{2,1,0:T(8,128)} custom-call(f32[2,4,512]{2,1,0:T(4,128)} %model_ref.1), custom_call_target="tpu_custom_call" | custom-call | tf_op jit(solution)/shard_map/gather/pallas_call | solution.py:390
  16.6 21.6 %block.1 = (f32[2,1,8192]{2,1,0:T(1,128)}, f32[16,16,128]{2,1,0:T(8,128)}) custom-call(s32[1,1,16]{2,1,0:T(1,128)} %listed_ref.1, f32[64,8,128]{2,1,0:T(8,128)} %gather.1.tiles_ref, f32[2,32,8]{2,1,0:T(8,128)} %copy.13.kernels_ref, f32[8,64,128]{2,1,0:T(8,128)} %constant.16.clone.rest_0_, f32[256,512]{1,0:T(8,128)} %constant.17.clone.rest_1_, ...), custom_call_target="tpu_custom_call" | custom-call | tf_op jit(solution)/shard_map/block/pallas_call | solution.py:351
  38.3 12.0 %back.1 = f32[2,4,512]{2,1,0:T(4,128)} custom-call(f32[16,16,128]{2,1,0:T(8,128)} %get-tuple-element.4.tiles_ref), custom_call_target="tpu_custom_call" | custom-call | tf_op jit(solution)/shard_map/back/pallas_call | solution.py:402
  50.3 0.7 %add_multiply_fusion.1 = (f32[1,4,512]{2,1,0:T(4,128)S(1)}, f32[1,4,512]{2,1,0:T(4,128)S(1)}) fusion(f32[2,4,512]{2,1,0:T(4,128)} %back.1), kind=kLoop, calls=%fused_computation.2 | loop fusion | flops 12288 | bytes 32768 | tf_op jit(solution)/shard_map/div | solution.py:412
  51.0 0.6 %pad_maximum_fusion = f32[2,4,512]{2,1,0:T(4,128)} fusion(f32[1,4,512]{2,1,0:T(4,128)S(1)} %get-tuple-element.7, f32[1,4,512]{2,1,0:T(4,128)S(1)} %get-tuple-element.6), kind=kLoop, calls=%fused_computation | loop fusion | flops 4096 | bytes 32768 | tf_op jit(solution)/shard_map/stack | solution.py:414
